TPU v7x, 32 devices: a whole 2x2x4 slice. The times are simulated.
32 devices in a mesh: gx: 2 (over y), gy: 4 (over x, core), gz: 4 (over z).
Axes of the slice: x: 2, y: 2, z: 4, core: 2. Of those that a mesh axis runs over, the one named last changes fastest.
Arguments:
- species: float32 [16, 16, 16, 654], P('gx', 'gy', 'gz'), may hold values from -6 to 6
- counts: int32 [16, 16, 16], P('gx', 'gy', 'gz'), may hold values from 1 to 8, as said below
- assignment: int32 [16, 16, 16], P('gx', 'gy', 'gz'), may hold values from 0 to 7, as said below
- cell_scale: float32 [16, 16, 16], P('gx', 'gy', 'gz'), may hold values from 0.5 to 1
- diffusivity: float32 [654], replicated, may hold values from 0.02 to 0.16
- order_weights: bfloat16 [654, 1536], replicated, may hold values from -0.25 to 0.25
- stoichiometry: bfloat16 [1536, 654], replicated, may hold values from -0.15625 to 0.15625
- rate_factor: float32 [1536], replicated, may hold values from 0.3 to 3
- enthalpy: float32 [654], replicated, may hold values from -4 to 4
Outputs:
- advanced: float32 [16, 16, 16, 654], P('gx', 'gy', 'gz')
- worker_heat: float32 [2, 4, 4], P('gx', 'gy', 'gz')
Inputs may be any that keep to these rules, and one draw needn't show every extreme that they name: `counts`: cells with many substeps cluster in one region of the grid. `assignment`: among the 128 cells of each device, exactly 16 are assigned to each device of its gx-gy plane.
All inputs are finite; a program needn't handle non-finite values.
Results may differ from a plain program's by a relative error of at most 0.0025.
Values sent between devices are 32-bit elements; how exact they have to be, the bound alone decides.
A program may use at most 64 MiB of HBM per device.

v0:
```python
import jax
import jax.numpy as jnp
from jax import lax
from jax.sharding import PartitionSpec as P

MAXSUB = 8
BLK = 128


relax_rate = 0.25


def extended(block, sides, width):
    for axis, dim in sides:
        count = lax.axis_size(axis)
        forward = [(i, i + 1) for i in range(count - 1)]
        backward = [(target, source) for source, target in forward]
        low = lax.ppermute(
            lax.slice_in_dim(block, block.shape[dim] - width, None, axis=dim), axis, forward
        )
        high = lax.ppermute(lax.slice_in_dim(block, 0, width, axis=dim), axis, backward)
        block = jnp.concatenate([low, block, high], axis=dim)
    return block


def section(state_now, cell_scale, diffusivity):
    padded = extended(state_now, (("gx", 0), ("gy", 1), ("gz", 2)), 1)
    beside_all = padded[2:, 1:-1, 1:-1] + padded[:-2, 1:-1, 1:-1]
    beside_all = beside_all + padded[1:-1, 2:, 1:-1] + padded[1:-1, :-2, 1:-1]
    beside_all = beside_all + padded[1:-1, 1:-1, 2:] + padded[1:-1, 1:-1, :-2]
    return state_now + cell_scale[..., None] * diffusivity * (beside_all - 6.0 * state_now)


def substep(tile_rows, order_weights, stoichiometry, rate_factor):
    activity = jnp.dot(
        tile_rows.astype(jnp.bfloat16), order_weights, preferred_element_type=jnp.float32
    )
    rate_values = (rate_factor * jax.nn.softplus(activity)).astype(jnp.bfloat16)
    change = jnp.dot(rate_values, stoichiometry, preferred_element_type=jnp.float32)
    return tile_rows + relax_rate * (change - tile_rows)


def advance(cell_rows, cell_counts, order_weights, stoichiometry, rate_factor, enthalpy):
    row_total = cell_rows.shape[0]
    positions = jnp.arange(row_total, dtype=jnp.int32)
    scores = (MAXSUB - cell_counts) * row_total + positions
    ordering = jnp.argsort(scores, stable=True)
    sorted_rows = cell_rows[ordering]
    sorted_counts = cell_counts[ordering]
    heat_rows = jnp.zeros((row_total,), jnp.float32)
    for substep_no in range(MAXSUB):
        live_rows = jnp.sum((sorted_counts > substep_no).astype(jnp.int32))
        block_count = (live_rows + BLK - 1) // BLK

        def advance_block(index, carried, substep_no=substep_no):
            rows_now, heat_now = carried
            tile_rows = rows_now
            tile_heat = heat_now
            stepped = substep(tile_rows, order_weights, stoichiometry, rate_factor)
            active = sorted_counts > substep_no
            released = jnp.sum(enthalpy * (tile_rows - stepped), axis=1)
            tile_heat = tile_heat + jnp.where(active, released, jnp.float32(0.0))
            tile_rows = jnp.where(active[:, None], stepped, tile_rows)
            rows_now = tile_rows
            heat_now = tile_heat
            return (rows_now, heat_now)

        sorted_rows, heat_rows = lax.fori_loop(
            0, block_count, advance_block, (sorted_rows, heat_rows)
        )
    inverse = jnp.zeros((row_total,), jnp.int32).at[ordering].set(positions)
    return (sorted_rows[inverse], heat_rows[inverse])


def local(
    species,
    counts,
    assignment,
    cell_scale,
    diffusivity,
    order_weights,
    stoichiometry,
    rate_factor,
    enthalpy,
):
    state_now = section(species, cell_scale, diffusivity)
    state_now = section(state_now, cell_scale, diffusivity)
    span_gx = lax.axis_size("gx")
    span_gy = lax.axis_size("gy")
    group_size = span_gx * span_gy
    brick_shape = state_now.shape
    species_count = brick_shape[3]
    cell_count = brick_shape[0] * brick_shape[1] * brick_shape[2]
    cell_rows = state_now.reshape(cell_count, species_count)
    cell_counts = counts.reshape(cell_count)
    targets = assignment.reshape(cell_count)
    advanced_rows, heat_rows = advance(
        cell_rows, cell_counts, order_weights, stoichiometry, rate_factor, enthalpy
    )
    target_hits = targets[:, None] == jnp.arange(group_size, dtype=jnp.int32)[None, :]
    partial_heat = jnp.sum(jnp.where(target_hits, heat_rows[:, None], jnp.float32(0.0)), axis=0)
    own_heat = lax.psum_scatter(partial_heat, ("gx", "gy"), scatter_dimension=0, tiled=True)
    worker_heat = (own_heat / cell_count).reshape(1, 1, 1)
    advanced = advanced_rows.reshape(brick_shape)
    return (advanced, worker_heat)


def solution(mesh):
    placed = (
        P("gx", "gy", "gz", None),
        P("gx", "gy", "gz"),
        P("gx", "gy", "gz"),
        P("gx", "gy", "gz"),
        P(),
        P(),
        P(),
        P(),
        P(),
    )
    return jax.shard_map(
        local,
        mesh=mesh,
        in_specs=placed,
        out_specs=(P("gx", "gy", "gz", None), P("gx", "gy", "gz")),
        check_vma=False,
    )
```

profile of v0, /device:TPU:0, one launch (start us, length us, event | category | flops | bytes accessed | tf_op | source)
XLA Modules:
  0.0 104.7 jit_solution(4385239773108790950)
XLA Ops:
  0.6 1.2 %copy.39 = f32[8,4,4,654]{3,0,2,1:T(8,128)S(1)} copy(f32[8,4,4,654]{3,2,1,0:T(4,128)} %param.25) | data formatting | bytes 669696 | tf_op args[0]
  1.9 0.1 fusion.153
  2.0 1.3 %collective-permute-start = (f32[1,4,4,654]{3,0,2,1:T(1,128)S(1)}, f32[1,4,4,654]{3,0,2,1:T(1,128)S(1)}, u32[]{:S(2)}, u32[]{:S(2)}) collective-permute-start(f32[1,4,4,654]{3,0,2,1:T(1,128)S(1)} %get-tuple-element.627), channel_id=1, source_target_pairs={{16,0},{17,1},{18,2},{19,3},{20,4},{21,5},{22,6},{23,7},{24,8},{25... | collective-permute-start | bytes 125576 | tf_op jit(solution)/shard_map/ppermute | solution.py:21
  3.3 4.9 %collective-permute-start.1 = (f32[1,4,4,654]{3,0,2,1:T(1,128)S(1)}, f32[1,4,4,654]{3,0,2,1:T(1,128)S(1)}, u32[]{:S(2)}, u32[]{:S(2)}) collective-permute-start(f32[1,4,4,654]{3,0,2,1:T(1,128)S(1)} %get-tuple-element.626), channel_id=1, source_target_pairs={{0,16},{1,17},{2,18},{3,19},{4,20},{5,21},{6,22},{7,23},{8,24},{9,... | collective-permute-start | bytes 125576 | tf_op jit(solution)/shard_map/ppermute | solution.py:18
  8.1 0.8 copy.41
  8.9 0.1 reshape.61
  9.1 0.8 collective-permute-done.1
  9.9 0.1 pad_maximum_fusion.49
  10.0 1.3 %collective-permute-start.2 = (f32[10,1,4,654]{3,0,2,1:T(8,128)S(1)}, f32[10,1,4,654]{3,0,2,1:T(8,128)S(1)}, u32[]{:S(2)}, u32[]{:S(2)}) collective-permute-start(f32[10,1,4,654]{3,0,2,1:T(8,128)S(1)} %get-tuple-element.623), channel_id=1, source_target_pairs={{4,0},{8,4},{12,8},{5,1},{9,5},{13,9},{6,2},{10,6},{14,10},{7,3},{... | collective-permute-start | bytes 313928 | tf_op jit(solution)/shard_map/ppermute | solution.py:21
  11.3 3.0 %collective-permute-start.3 = (f32[10,1,4,654]{3,0,2,1:T(8,128)S(1)}, f32[10,1,4,654]{3,0,2,1:T(8,128)S(1)}, u32[]{:S(2)}, u32[]{:S(2)}) collective-permute-start(f32[10,1,4,654]{3,0,2,1:T(8,128)S(1)} %get-tuple-element.622), channel_id=1, source_target_pairs={{0,4},{4,8},{8,12},{1,5},{5,9},{9,13},{2,6},{6,10},{10,14},{3,7},{... | collective-permute-start | bytes 313928 | tf_op jit(solution)/shard_map/ppermute | solution.py:18
  14.3 2.5 %sort.17 = (s32[128]{0:T(128)}, s32[128]{0:T(128)S(1)}) sort(s32[128]{0:T(128)S(1)} %iota_add_fusion, s32[128]{0:T(128)S(1)} %iota.14), dimensions={0}, to_apply=%region_0.0 | sort | flops 896 | bytes 2048 | tf_op jit(solution)/shard_map/jit(argsort)/sort | solution.py:47
  16.9 0.1 pad_maximum_fusion.45
  17.0 1.3 %collective-permute-start.4 = (f32[10,6,1,654]{3,0,2,1:T(8,128)S(1)}, f32[10,6,1,654]{3,0,2,1:T(8,128)S(1)}, u32[]{:S(2)}, u32[]{:S(2)}) collective-permute-start(f32[10,6,1,654]{3,0,2,1:T(8,128)S(1)} %get-tuple-element.618), channel_id=1, source_target_pairs={{1,0},{2,1},{3,2},{5,4},{6,5},{7,6},{9,8},{10,9},{11,10},{13,12},{... | collective-permute-start | bytes 470888 | tf_op jit(solution)/shard_map/ppermute | solution.py:21
  18.3 5.2 %collective-permute-start.5 = (f32[10,6,1,654]{3,0,2,1:T(8,128)S(1)}, f32[10,6,1,654]{3,0,2,1:T(8,128)S(1)}, u32[]{:S(2)}, u32[]{:S(2)}) collective-permute-start(f32[10,6,1,654]{3,0,2,1:T(8,128)S(1)} %get-tuple-element.619), channel_id=1, source_target_pairs={{0,1},{1,2},{2,3},{4,5},{5,6},{6,7},{8,9},{9,10},{10,11},{12,13},{... | collective-permute-start | bytes 470888 | tf_op jit(solution)/shard_map/ppermute | solution.py:18
  23.5 1.0 scatter_custom_fusion
  24.5 4.4 %collective-permute-done.4 = f32[10,6,1,654]{3,0,2,1:T(8,128)S(1)} collective-permute-done((f32[10,6,1,654]{3,0,2,1:T(8,128)S(1)}, f32[10,6,1,654]{3,0,2,1:T(8,128)S(1)}, u32[]{:S(2)}, u32[]{:S(2)}) %collective-permute-start.4) | collective-permute-done | bytes 156992 | tf_op jit(solution)/shard_map/ppermute | solution.py:21
  28.9 1.7 %collective-permute-done.5 = f32[10,6,1,654]{3,0,2,1:T(8,128)S(1)} collective-permute-done((f32[10,6,1,654]{3,0,2,1:T(8,128)S(1)}, f32[10,6,1,654]{3,0,2,1:T(8,128)S(1)}, u32[]{:S(2)}, u32[]{:S(2)}) %collective-permute-start.5) | collective-permute-done | bytes 156992 | tf_op jit(solution)/shard_map/ppermute | solution.py:18
  30.6 0.4 fusion.112
  30.9 0.0 copy-start.6
  31.0 0.1 fusion.152
  31.0 1.3 %collective-permute-start.6 = (f32[1,4,4,654]{3,0,2,1:T(1,128)S(1)}, f32[1,4,4,654]{3,0,2,1:T(1,128)S(1)}, u32[]{:S(2)}, u32[]{:S(2)}) collective-permute-start(f32[1,4,4,654]{3,0,2,1:T(1,128)S(1)} %get-tuple-element.625), channel_id=1, source_target_pairs={{16,0},{17,1},{18,2},{19,3},{20,4},{21,5},{22,6},{23,7},{24,8},{25... | collective-permute-start | bytes 125576 | tf_op jit(solution)/shard_map/ppermute | solution.py:21
  32.3 4.5 %collective-permute-start.7 = (f32[1,4,4,654]{3,0,2,1:T(1,128)S(1)}, f32[1,4,4,654]{3,0,2,1:T(1,128)S(1)}, u32[]{:S(2)}, u32[]{:S(2)}) collective-permute-start(f32[1,4,4,654]{3,0,2,1:T(1,128)S(1)} %get-tuple-element.624), channel_id=1, source_target_pairs={{0,16},{1,17},{2,18},{3,19},{4,20},{5,21},{6,22},{7,23},{8,24},{9,... | collective-permute-start | bytes 125576 | tf_op jit(solution)/shard_map/ppermute | solution.py:18
  36.9 0.1 collective-permute-done.6
  37.0 1.6 %collective-permute-done.7 = f32[1,4,4,654]{3,0,2,1:T(1,128)S(1)} collective-permute-done((f32[1,4,4,654]{3,0,2,1:T(1,128)S(1)}, f32[1,4,4,654]{3,0,2,1:T(1,128)S(1)}, u32[]{:S(2)}, u32[]{:S(2)}) %collective-permute-start.7) | collective-permute-done | bytes 41888 | tf_op jit(solution)/shard_map/ppermute | solution.py:18
  38.6 0.1 pad_maximum_fusion.46
  38.7 1.3 %collective-permute-start.8 = (f32[10,1,4,654]{3,0,2,1:T(8,128)S(1)}, f32[10,1,4,654]{3,0,2,1:T(8,128)S(1)}, u32[]{:S(2)}, u32[]{:S(2)}) collective-permute-start(f32[10,1,4,654]{3,0,2,1:T(8,128)S(1)} %get-tuple-element.621), channel_id=1, source_target_pairs={{4,0},{8,4},{12,8},{5,1},{9,5},{13,9},{6,2},{10,6},{14,10},{7,3},{... | collective-permute-start | bytes 313928 | tf_op jit(solution)/shard_map/ppermute | solution.py:21
  40.0 3.0 %collective-permute-start.9 = (f32[10,1,4,654]{3,0,2,1:T(8,128)S(1)}, f32[10,1,4,654]{3,0,2,1:T(8,128)S(1)}, u32[]{:S(2)}, u32[]{:S(2)}) collective-permute-start(f32[10,1,4,654]{3,0,2,1:T(8,128)S(1)} %get-tuple-element.620), channel_id=1, source_target_pairs={{0,4},{4,8},{8,12},{1,5},{5,9},{9,13},{2,6},{6,10},{10,14},{3,7},{... | collective-permute-start | bytes 313928 | tf_op jit(solution)/shard_map/ppermute | solution.py:18
  43.1 1.2 %gather_fusion.1 = s32[128]{0:T(128)S(1)} fusion(s32[128]{0:T(128)S(1)} %reshape.61, s32[1024]{0:T(1024)S(1)} %pad_clamp_fusion.1), kind=kCustom, calls=%fused_computation.1 | custom fusion | bytes 1536 | tf_op jit(solution)/shard_map/gather | solution.py:49
  44.3 0.1 pad_maximum_fusion.40
  44.4 1.3 %collective-permute-start.10 = (f32[10,6,1,654]{3,0,2,1:T(8,128)S(1)}, f32[10,6,1,654]{3,0,2,1:T(8,128)S(1)}, u32[]{:S(2)}, u32[]{:S(2)}) collective-permute-start(f32[10,6,1,654]{3,0,2,1:T(8,128)S(1)} %get-tuple-element.616), channel_id=1, source_target_pairs={{1,0},{2,1},{3,2},{5,4},{6,5},{7,6},{9,8},{10,9},{11,10},{13,12},{... | collective-permute-start | bytes 470888 | tf_op jit(solution)/shard_map/ppermute | solution.py:21
  45.7 5.0 %collective-permute-start.11 = (f32[10,6,1,654]{3,0,2,1:T(8,128)S(1)}, f32[10,6,1,654]{3,0,2,1:T(8,128)S(1)}, u32[]{:S(2)}, u32[]{:S(2)}) collective-permute-start(f32[10,6,1,654]{3,0,2,1:T(8,128)S(1)} %get-tuple-element.617), channel_id=1, source_target_pairs={{0,1},{1,2},{2,3},{4,5},{5,6},{6,7},{8,9},{9,10},{10,11},{12,13},{... | collective-permute-start | bytes 470888 | tf_op jit(solution)/shard_map/ppermute | solution.py:18
  50.7 0.8 fusion.133
  56.7 0.1 copy.44
  56.8 0.1 eq.15
  57.0 0.6 dynamic-slice
  57.6 0.4 fusion.113
  58.0 0.2 copy.40
  58.2 0.1 reshape.60
  58.4 0.8 gather_fusion
  59.2 0.2 copy.42
  59.4 0.5 copy-done.3
  59.9 3.1 %while.96 = (s32[]{:T(128)}, f32[128,654]{0,1:T(8,128)S(1)}, f32[128]{0:T(128)S(1)}, s32[]{:T(128)}, s32[128]{0:T(128)S(1)}, /*index=5*/f32[1536]{0:T(1024)S(1)}...) while((s32[]{:T(128)}, f32[128,654]{0,1:T(8,128)S(1)}, ...), condition=%wide.region_4.5_spmd, body=%wide.region_2.4_spmd.sunk | while | flops 516569472 | bytes 5369757 | solution.py:68
  59.9 3.0 %multiply_reduce_fusion.16 = (f32[128]{0:T(128)S(1)}, f32[128,654]{0,1:T(8,128)S(1)}) fusion(f32[128,654]{0,1:T(8,128)S(1)} %copy.126, f32[654]{0:T(1024)S(1)} %get-tuple-element.1136, pred[128]{0:T(512)(128)(4,1)S(1)} %broadcast_compare_fusion.16, bf16[1536,654]{0,1:T(8,128)(2,1)} %get-tuple-element.1135, f32[1536]{0:T(1024)S(1)} %get-tuple-element.1133, ...), kind=kOutput, calls=%fused_computation.13.clone.1 | convolution fusion | flops 516568960 | bytes 4697272 | tf_op jit(solution)/shard_map/while/body/dot_general | solution.py:39
  63.0 3.1 %while.97 = (s32[]{:T(128)}, f32[128,654]{0,1:T(8,128)S(1)}, f32[128]{0:T(128)S(1)}, s32[]{:T(128)}, s32[128]{0:T(128)S(1)}, /*index=5*/f32[1536]{0:T(1024)S(1)}...) while((s32[]{:T(128)}, f32[128,654]{0,1:T(8,128)S(1)}, ...), condition=%wide.region_8.9_spmd, body=%wide.region_6.8_spmd.sunk | while | flops 516569472 | bytes 5369757 | solution.py:68
  63.1 3.0 %multiply_reduce_fusion.17 = (f32[128]{0:T(128)S(1)}, f32[128,654]{0,1:T(8,128)S(1)}) fusion(f32[128,654]{0,1:T(8,128)S(1)} %copy.127, f32[654]{0:T(1024)S(1)} %get-tuple-element.1166, pred[128]{0:T(512)(128)(4,1)S(1)} %broadcast_compare_fusion.17, bf16[1536,654]{0,1:T(8,128)(2,1)} %get-tuple-element.1165, f32[1536]{0:T(1024)S(1)} %get-tuple-element.1163, ...), kind=kOutput, calls=%fused_computation.28.clone.1 | convolution fusion | flops 516568960 | bytes 4697272 | tf_op jit(solution)/shard_map/while/body/dot_general | solution.py:39
  66.1 3.1 %while.98 = (s32[]{:T(128)}, f32[128,654]{0,1:T(8,128)S(1)}, f32[128]{0:T(128)S(1)}, s32[]{:T(128)}, s32[128]{0:T(128)S(1)}, /*index=5*/f32[1536]{0:T(1024)S(1)}...) while((s32[]{:T(128)}, f32[128,654]{0,1:T(8,128)S(1)}, ...), condition=%wide.region_12.13_spmd, body=%wide.region_10.12_spmd.sunk | while | flops 516569472 | bytes 5369757 | solution.py:68
  66.2 3.0 %multiply_reduce_fusion.18 = (f32[128]{0:T(128)S(1)}, f32[128,654]{0,1:T(8,128)S(1)}) fusion(f32[128,654]{0,1:T(8,128)S(1)} %copy.128, f32[654]{0:T(1024)S(1)} %get-tuple-element.1196, pred[128]{0:T(512)(128)(4,1)S(1)} %broadcast_compare_fusion.18, bf16[1536,654]{0,1:T(8,128)(2,1)} %get-tuple-element.1195, f32[1536]{0:T(1024)S(1)} %get-tuple-element.1193, ...), kind=kOutput, calls=%fused_computation.43.clone.1 | convolution fusion | flops 516568960 | bytes 4697272 | tf_op jit(solution)/shard_map/while/body/dot_general | solution.py:39
  69.2 3.1 %while.99 = (s32[]{:T(128)}, f32[128,654]{0,1:T(8,128)S(1)}, f32[128]{0:T(128)S(1)}, s32[]{:T(128)}, s32[128]{0:T(128)S(1)}, /*index=5*/f32[1536]{0:T(1024)S(1)}...) while((s32[]{:T(128)}, f32[128,654]{0,1:T(8,128)S(1)}, ...), condition=%wide.region_16.17_spmd, body=%wide.region_14.16_spmd.sunk | while | flops 516569472 | bytes 5369757 | solution.py:68
  69.3 3.0 %multiply_reduce_fusion.19 = (f32[128]{0:T(128)S(1)}, f32[128,654]{0,1:T(8,128)S(1)}) fusion(f32[128,654]{0,1:T(8,128)S(1)} %copy.129, f32[654]{0:T(1024)S(1)} %get-tuple-element.1226, pred[128]{0:T(512)(128)(4,1)S(1)} %broadcast_compare_fusion.19, bf16[1536,654]{0,1:T(8,128)(2,1)} %get-tuple-element.1225, f32[1536]{0:T(1024)S(1)} %get-tuple-element.1223, ...), kind=kOutput, calls=%fused_computation.58.clone.1 | convolution fusion | flops 516568960 | bytes 4697272 | tf_op jit(solution)/shard_map/while/body/dot_general | solution.py:39
  72.4 3.1 %while.100 = (s32[]{:T(128)}, f32[128,654]{0,1:T(8,128)S(1)}, f32[128]{0:T(128)S(1)}, s32[]{:T(128)}, s32[128]{0:T(128)S(1)}, /*index=5*/f32[1536]{0:T(1024)S(1)...) while((s32[]{:T(128)}, f32[128,654]{0,1:T(8,128)S(1)}, ...), condition=%wide.region_20.21_spmd, body=%wide.region_18.20_spmd.sunk | while | flops 516569472 | bytes 5369757 | solution.py:68
  72.4 3.0 %multiply_reduce_fusion.20 = (f32[128]{0:T(128)S(1)}, f32[128,654]{0,1:T(8,128)S(1)}) fusion(f32[128,654]{0,1:T(8,128)S(1)} %copy.130, f32[654]{0:T(1024)S(1)} %get-tuple-element.1256, pred[128]{0:T(512)(128)(4,1)S(1)} %broadcast_compare_fusion.20, bf16[1536,654]{0,1:T(8,128)(2,1)} %get-tuple-element.1255, f32[1536]{0:T(1024)S(1)} %get-tuple-element.1253, ...), kind=kOutput, calls=%fused_computation.73.clone.1 | convolution fusion | flops 516568960 | bytes 4697272 | tf_op jit(solution)/shard_map/while/body/dot_general | solution.py:39
  75.5 3.3 %while.101 = (s32[]{:T(128)}, f32[128,654]{0,1:T(8,128)S(1)}, f32[128]{0:T(128)S(1)}, s32[]{:T(128)}, s32[128]{0:T(128)S(1)}, /*index=5*/f32[1536]{0:T(1024)S(1)...) while((s32[]{:T(128)}, f32[128,654]{0,1:T(8,128)S(1)}, ...), condition=%wide.region_24.25_spmd, body=%wide.region_22.24_spmd.sunk | while | flops 516569472 | bytes 5369757 | solution.py:68
  75.7 3.0 %multiply_reduce_fusion.21 = (f32[128]{0:T(128)S(1)}, f32[128,654]{0,1:T(8,128)S(1)}) fusion(f32[128,654]{0,1:T(8,128)S(1)} %copy.131, f32[654]{0:T(1024)S(1)} %get-tuple-element.1286, pred[128]{0:T(512)(128)(4,1)S(1)} %broadcast_compare_fusion.21, bf16[1536,654]{0,1:T(8,128)(2,1)} %get-tuple-element.1285, f32[1536]{0:T(1024)S(1)} %get-tuple-element.1283, ...), kind=kOutput, calls=%fused_computation.88.clone.1 | convolution fusion | flops 516568960 | bytes 4697272 | tf_op jit(solution)/shard_map/while/body/dot_general | solution.py:39
  78.8 3.1 %while.102 = (s32[]{:T(128)}, f32[128,654]{0,1:T(8,128)S(1)}, f32[128]{0:T(128)S(1)}, s32[]{:T(128)}, s32[128]{0:T(128)S(1)}, /*index=5*/f32[1536]{0:T(1024)S(1)...) while((s32[]{:T(128)}, f32[128,654]{0,1:T(8,128)S(1)}, ...), condition=%wide.region_28.29_spmd, body=%wide.region_26.28_spmd.sunk | while | flops 516569472 | bytes 5369757 | solution.py:68
  78.9 3.0 %multiply_reduce_fusion.22 = (f32[128]{0:T(128)S(1)}, f32[128,654]{0,1:T(8,128)S(1)}) fusion(f32[128,654]{0,1:T(8,128)S(1)} %copy.132, f32[654]{0:T(1024)S(1)} %get-tuple-element.1316, pred[128]{0:T(512)(128)(4,1)S(1)} %broadcast_compare_fusion.22, bf16[1536,654]{0,1:T(8,128)(2,1)} %get-tuple-element.1315, f32[1536]{0:T(1024)S(1)} %get-tuple-element.1313, ...), kind=kOutput, calls=%fused_computation.103.clone.1 | convolution fusion | flops 516568960 | bytes 4697272 | tf_op jit(solution)/shard_map/while/body/dot_general | solution.py:39
  81.9 3.1 %while.103 = (s32[]{:T(128)}, f32[128,654]{0,1:T(8,128)S(1)}, f32[128]{0:T(128)S(1)}, s32[]{:T(128)}, s32[128]{0:T(128)S(1)}, /*index=5*/f32[1536]{0:T(1024)S(1)...) while((s32[]{:T(128)}, f32[128,654]{0,1:T(8,128)S(1)}, ...), condition=%wide.region_32.33_spmd, body=%wide.region_30.32_spmd.sunk | while | flops 516569472 | bytes 5369757 | solution.py:68
  82.0 3.0 %multiply_reduce_fusion.23 = (f32[128]{0:T(128)S(1)}, f32[128,654]{0,1:T(8,128)S(1)}) fusion(f32[128,654]{0,1:T(8,128)S(1)} %copy.133, f32[654]{0:T(1024)S(1)} %get-tuple-element.1346, pred[128]{0:T(512)(128)(4,1)S(1)} %broadcast_compare_fusion.23, bf16[1536,654]{0,1:T(8,128)(2,1)} %get-tuple-element.1345, f32[1536]{0:T(1024)S(1)} %get-tuple-element.1343, ...), kind=kOutput, calls=%fused_computation.118.clone.1 | convolution fusion | flops 516568960 | bytes 4697272 | tf_op jit(solution)/shard_map/while/body/dot_general | solution.py:39
  85.0 0.2 copy.43
  85.2 0.8 gather_fusion.2
  86.0 1.2 %gather_fusion.3 = f32[128]{0:T(128)S(1)} fusion(f32[128]{0:T(128)S(1)} %get-tuple-element.411, s32[1024]{0:T(1024)S(1)} %pad_clamp_fusion), kind=kCustom, calls=%fused_computation.3 | custom fusion | bytes 1536 | tf_op jit(solution)/shard_map/gather | solution.py:72
  87.3 0.1 select_reduce_fusion
  87.4 0.9 reshape.62
  88.2 13.5 %all-reduce = f32[8]{0:T(128)S(1)} all-reduce(f32[8]{0:T(128)S(1)} %select_reduce_fusion), channel_id=2, replica_groups=mesh['gx'=2,'gy'=4,'gz'=4] {'gx','gy'}, use_global_device_ids=true, to_apply=%region_35.36.clone | all-reduce | flops 8 | bytes 64
  101.7 1.1 %dynamic-slice.1 = f32[1]{0:T(128)} dynamic-slice(f32[8]{0:T(128)S(1)} %all-reduce, u32[]{:T(128)} %bitcast.1), dynamic_slice_sizes={1} | dynamic-slice | bytes 12
  (51 shorter events, 0.4 us)
Async XLA Ops:
  0.6 29.9 %copy-start = (f32[8,4,4]{0,2,1:T(4,128)S(1)}, f32[8,4,4]{0,2,1:T(4,128)}, u32[]{:S(2)}) copy-start(f32[8,4,4]{0,2,1:T(4,128)} %param.28) | copy-start | bytes 1540
  0.6 29.9 %copy-start.1 = (f32[654]{0:T(1024)S(1)}, f32[654]{0:T(1024)}, u32[]{:S(2)}) copy-start(f32[654]{0:T(1024)} %param.29) | copy-start | bytes 7852
  2.0 7.1 %collective-permute-start = (f32[1,4,4,654]{3,0,2,1:T(1,128)S(1)}, f32[1,4,4,654]{3,0,2,1:T(1,128)S(1)}, u32[]{:S(2)}, u32[]{:S(2)}) collective-permute-start(f32[1,4,4,654]{3,0,2,1:T(1,128)S(1)} %get-tuple-element.627), channel_id=1, source_target_pairs={{16,0},{17,1},{18,2},{19,3},{20,4},{21,5},{22,6},{23,7},{24,8},{25... | collective-permute-start | bytes 125576 | tf_op jit(solution)/shard_map/ppermute | solution.py:21
  3.3 6.6 %collective-permute-start.1 = (f32[1,4,4,654]{3,0,2,1:T(1,128)S(1)}, f32[1,4,4,654]{3,0,2,1:T(1,128)S(1)}, u32[]{:S(2)}, u32[]{:S(2)}) collective-permute-start(f32[1,4,4,654]{3,0,2,1:T(1,128)S(1)} %get-tuple-element.626), channel_id=1, source_target_pairs={{0,16},{1,17},{2,18},{3,19},{4,20},{5,21},{6,22},{7,23},{8,24},{9,... | collective-permute-start | bytes 125576 | tf_op jit(solution)/shard_map/ppermute | solution.py:18
  10.0 6.9 %collective-permute-start.2 = (f32[10,1,4,654]{3,0,2,1:T(8,128)S(1)}, f32[10,1,4,654]{3,0,2,1:T(8,128)S(1)}, u32[]{:S(2)}, u32[]{:S(2)}) collective-permute-start(f32[10,1,4,654]{3,0,2,1:T(8,128)S(1)} %get-tuple-element.623), channel_id=1, source_target_pairs={{4,0},{8,4},{12,8},{5,1},{9,5},{13,9},{6,2},{10,6},{14,10},{7,3},{... | collective-permute-start | bytes 313928 | tf_op jit(solution)/shard_map/ppermute | solution.py:21
  11.3 5.6 %collective-permute-start.3 = (f32[10,1,4,654]{3,0,2,1:T(8,128)S(1)}, f32[10,1,4,654]{3,0,2,1:T(8,128)S(1)}, u32[]{:S(2)}, u32[]{:S(2)}) collective-permute-start(f32[10,1,4,654]{3,0,2,1:T(8,128)S(1)} %get-tuple-element.622), channel_id=1, source_target_pairs={{0,4},{4,8},{8,12},{1,5},{5,9},{9,13},{2,6},{6,10},{10,14},{3,7},{... | collective-permute-start | bytes 313928 | tf_op jit(solution)/shard_map/ppermute | solution.py:18
  17.0 11.9 %collective-permute-start.4 = (f32[10,6,1,654]{3,0,2,1:T(8,128)S(1)}, f32[10,6,1,654]{3,0,2,1:T(8,128)S(1)}, u32[]{:S(2)}, u32[]{:S(2)}) collective-permute-start(f32[10,6,1,654]{3,0,2,1:T(8,128)S(1)} %get-tuple-element.618), channel_id=1, source_target_pairs={{1,0},{2,1},{3,2},{5,4},{6,5},{7,6},{9,8},{10,9},{11,10},{13,12},{... | collective-permute-start | bytes 470888 | tf_op jit(solution)/shard_map/ppermute | solution.py:21
  18.3 12.3 %collective-permute-start.5 = (f32[10,6,1,654]{3,0,2,1:T(8,128)S(1)}, f32[10,6,1,654]{3,0,2,1:T(8,128)S(1)}, u32[]{:S(2)}, u32[]{:S(2)}) collective-permute-start(f32[10,6,1,654]{3,0,2,1:T(8,128)S(1)} %get-tuple-element.619), channel_id=1, source_target_pairs={{0,1},{1,2},{2,3},{4,5},{5,6},{6,7},{8,9},{9,10},{10,11},{12,13},{... | collective-permute-start | bytes 470888 | tf_op jit(solution)/shard_map/ppermute | solution.py:18
  30.9 25.8 %copy-start.2 = (s32[8,4,4]{0,2,1:T(4,128)S(1)}, s32[8,4,4]{0,2,1:T(4,128)}, u32[]{:S(2)}) copy-start(s32[8,4,4]{0,2,1:T(4,128)} %param.27) | copy-start | bytes 1540
  30.9 26.1 %copy-start.6 = (u32[32]{0:T(128)S(1)}, u32[32]{0:T(128)}, u32[]{:S(2)}) copy-start(u32[32]{0:T(128)} %constant.182) | copy-start | bytes 388
  31.0 6.0 %collective-permute-start.6 = (f32[1,4,4,654]{3,0,2,1:T(1,128)S(1)}, f32[1,4,4,654]{3,0,2,1:T(1,128)S(1)}, u32[]{:S(2)}, u32[]{:S(2)}) collective-permute-start(f32[1,4,4,654]{3,0,2,1:T(1,128)S(1)} %get-tuple-element.625), channel_id=1, source_target_pairs={{16,0},{17,1},{18,2},{19,3},{20,4},{21,5},{22,6},{23,7},{24,8},{25... | collective-permute-start | bytes 125576 | tf_op jit(solution)/shard_map/ppermute | solution.py:21
  32.3 6.3 %collective-permute-start.7 = (f32[1,4,4,654]{3,0,2,1:T(1,128)S(1)}, f32[1,4,4,654]{3,0,2,1:T(1,128)S(1)}, u32[]{:S(2)}, u32[]{:S(2)}) collective-permute-start(f32[1,4,4,654]{3,0,2,1:T(1,128)S(1)} %get-tuple-element.624), channel_id=1, source_target_pairs={{0,16},{1,17},{2,18},{3,19},{4,20},{5,21},{6,22},{7,23},{8,24},{9,... | collective-permute-start | bytes 125576 | tf_op jit(solution)/shard_map/ppermute | solution.py:18
  38.7 5.6 %collective-permute-start.8 = (f32[10,1,4,654]{3,0,2,1:T(8,128)S(1)}, f32[10,1,4,654]{3,0,2,1:T(8,128)S(1)}, u32[]{:S(2)}, u32[]{:S(2)}) collective-permute-start(f32[10,1,4,654]{3,0,2,1:T(8,128)S(1)} %get-tuple-element.621), channel_id=1, source_target_pairs={{4,0},{8,4},{12,8},{5,1},{9,5},{13,9},{6,2},{10,6},{14,10},{7,3},{... | collective-permute-start | bytes 313928 | tf_op jit(solution)/shard_map/ppermute | solution.py:21
  40.0 4.3 %collective-permute-start.9 = (f32[10,1,4,654]{3,0,2,1:T(8,128)S(1)}, f32[10,1,4,654]{3,0,2,1:T(8,128)S(1)}, u32[]{:S(2)}, u32[]{:S(2)}) collective-permute-start(f32[10,1,4,654]{3,0,2,1:T(8,128)S(1)} %get-tuple-element.620), channel_id=1, source_target_pairs={{0,4},{4,8},{8,12},{1,5},{5,9},{9,13},{2,6},{6,10},{10,14},{3,7},{... | collective-permute-start | bytes 313928 | tf_op jit(solution)/shard_map/ppermute | solution.py:18
  44.4 13.2 %collective-permute-start.10 = (f32[10,6,1,654]{3,0,2,1:T(8,128)S(1)}, f32[10,6,1,654]{3,0,2,1:T(8,128)S(1)}, u32[]{:S(2)}, u32[]{:S(2)}) collective-permute-start(f32[10,6,1,654]{3,0,2,1:T(8,128)S(1)} %get-tuple-element.616), channel_id=1, source_target_pairs={{1,0},{2,1},{3,2},{5,4},{6,5},{7,6},{9,8},{10,9},{11,10},{13,12},{... | collective-permute-start | bytes 470888 | tf_op jit(solution)/shard_map/ppermute | solution.py:21
  45.7 11.9 %collective-permute-start.11 = (f32[10,6,1,654]{3,0,2,1:T(8,128)S(1)}, f32[10,6,1,654]{3,0,2,1:T(8,128)S(1)}, u32[]{:S(2)}, u32[]{:S(2)}) collective-permute-start(f32[10,6,1,654]{3,0,2,1:T(8,128)S(1)} %get-tuple-element.617), channel_id=1, source_target_pairs={{0,1},{1,2},{2,3},{4,5},{5,6},{6,7},{8,9},{9,10},{10,11},{12,13},{... | collective-permute-start | bytes 470888 | tf_op jit(solution)/shard_map/ppermute | solution.py:18
  58.3 1.6 %copy-start.3 = (bf16[654,1536]{1,0:T(8,128)(2,1)S(1)}, bf16[654,1536]{1,0:T(8,128)(2,1)}, u32[]{:S(2)}) copy-start(bf16[654,1536]{1,0:T(8,128)(2,1)} %param.30) | copy-start | bytes 6027268
  58.3 1.6 %copy-start.4 = (f32[1536]{0:T(1024)S(1)}, f32[1536]{0:T(1024)}, u32[]{:S(2)}) copy-start(f32[1536]{0:T(1024)} %param.32) | copy-start | bytes 18436
  58.3 1.5 %copy-start.5 = (f32[654]{0:T(1024)S(1)}, f32[654]{0:T(1024)}, u32[]{:S(2)}) copy-start(f32[654]{0:T(1024)} %param.33) | copy-start | bytes 7852
where the time goes:
time: 106 us; the launch traced here: 105 us
  starting transfers between devices  33.5 us (32%)
  matrix products  24.3 us (23%)
  blocking collectives  13.5 us (13%)
  local copies, waits for them, and re-layouts  11.5 us (11%)
  waiting for transfers between devices  8.59 us (8%)
  between operations  8.09 us (8%)
  other arithmetic  4.69 us (4%)
    ppermute x6, starting transfers between devices, extended(): lax.ppermute(lax.slice_in_dim(block, block.shape[dim] - width, None, axis...  25.8 us
    dot_general x8, matrix products, substep(): jnp.dot(rate_values, stoichiometry, preferred_element_type=jnp.float32)  24.3 us
    unnamed x1, blocking collectives  13.5 us
    ppermute x6, starting transfers between devices, extended(): lax.ppermute(lax.slice_in_dim(block, 0, width, axis=dim), axis, backward)  7.75 us
    ppermute x6, waiting for transfers between devices, extended(): lax.ppermute(lax.slice_in_dim(block, 0, width, axis=dim), axis, backward)  4.5 us
    unnamed x19, local copies, waits for them, and re-layouts  4.44 us
    ppermute x6, waiting for transfers between devices, extended(): lax.ppermute(lax.slice_in_dim(block, block.shape[dim] - width, None, axis...  4.1 us
    sort x1, other arithmetic, advance(): ordering = jnp.argsort(scores, stable=True)  2.54 us
  transfers between devices with their start and end apart: 12, of which 5 were waited for; matrix products, arithmetic and copies ran while one was open for 7% of the time, Pallas kernels for 0%

commit v1 on v0

v1 whole, which is shorter than its diff:
```python
import jax
import jax.numpy as jnp
from jax import lax
from jax.experimental import pallas as pl
from jax.experimental.pallas import tpu as pltpu
from jax.sharding import PartitionSpec as P

MAXSUB = 8
relax_rate = 0.25
AXES = ("gx", "gy", "gz")
MESH = pl.DeviceIdType.MESH


def kernel(
    species,
    counts,
    assignment,
    cell_scale,
    diffusivity,
    order_weights,
    stoichiometry,
    rate_factor,
    enthalpy,
    advanced,
    worker_heat,
    weights_in,
    weights_out,
    weights_tail,
    weights_turned,
    halo_x,
    halo_y,
    halo_z,
    face_z,
    middle,
    rows,
    start_state,
    state,
    rates,
    factors,
    formation,
    cell_counts,
    cell_targets,
    heat_part,
    heat_all,
    load_sem,
    send_sem,
    recv_sem,
    heat_send,
    heat_recv,
):
    spans = [lax.axis_size(axis) for axis in AXES]
    here = [lax.axis_index(axis) for axis in AXES]
    span_y = spans[1]
    group = spans[0] * span_y
    me = here[0] * span_y + here[1]
    cx, cy, cz, width = species.shape
    cells = cx * cy * cz
    depth = order_weights.shape[1]

    loads = [
        pltpu.make_async_copy(order_weights, weights_in, load_sem.at[0]),
        pltpu.make_async_copy(stoichiometry, weights_out, load_sem.at[1]),
    ]
    for load in loads:
        load.start()

    def present(axis_no, side):
        if side == 0:
            return here[axis_no] > 0
        return here[axis_no] < spans[axis_no] - 1

    def peer(offset):
        target = lax.rem(me + offset, group)
        return {"gx": target // span_y, "gy": lax.rem(target, span_y)}

    barrier = pltpu.get_barrier_semaphore()
    for offset in range(1, group):
        pl.semaphore_signal(barrier, inc=1, device_id=peer(offset), device_id_type=MESH)
    for side in range(2):

        @pl.when(present(2, side))
        def _(side=side):
            pl.semaphore_signal(
                barrier, inc=1, device_id={"gz": here[2] + 2 * side - 1}, device_id_type=MESH
            )

    def face_copy(phase, axis_no, side, slot):
        block = species if phase == 0 else middle
        if axis_no == 0:
            source, halo = block.at[0 if side == 0 else cx - 1], halo_x
        elif axis_no == 1:
            source, halo = block.at[:, 0 if side == 0 else cy - 1], halo_y
        else:
            source, halo = face_z.at[phase, side], halo_z
        return pltpu.make_async_remote_copy(
            src_ref=source,
            dst_ref=halo.at[phase, slot],
            send_sem=send_sem.at[phase, axis_no, side],
            recv_sem=recv_sem.at[phase, axis_no, slot],
            device_id={AXES[axis_no]: here[axis_no] + 2 * side - 1},
            device_id_type=MESH,
        )

    def fill_face_z(phase):
        block = species if phase == 0 else middle
        face_z[phase, 0] = block[:, :, 0:1, :]
        face_z[phase, 1] = block[:, :, cz - 1 : cz, :]

    def each_face(action):
        for axis_no in (2, 1, 0):
            for side in range(2):

                @pl.when(present(axis_no, side))
                def _(axis_no=axis_no, side=side):
                    action(axis_no, side)

    fill_face_z(0)
    for phase in range(2):
        for side in range(2):
            for axis_no, halo in enumerate((halo_x, halo_y, halo_z)):

                @pl.when(jnp.logical_not(present(axis_no, side)))
                def _(phase=phase, side=side, halo=halo):
                    halo[phase, side] = jnp.zeros(halo.shape[2:], jnp.float32)

    pl.semaphore_wait(
        barrier,
        group - 1 + present(2, 0).astype(jnp.int32) + present(2, 1).astype(jnp.int32),
    )
    each_face(lambda axis_no, side: face_copy(0, axis_no, side, 1 - side).start())

    rows[...] = jnp.zeros(rows.shape, jnp.float32)
    for source, target in ((counts, cell_counts), (assignment, cell_targets)):
        for x in range(cx):
            for y in range(cy):
                first = x * cy * cz + y * cz
                column = source[y][:, x : x + 1].astype(jnp.float32)
                rows[first : first + cz, :cells] = jnp.broadcast_to(column, (cz, cells))
        target[...] = rows[:, :cells].T[:1]
    padded = rows.shape[1]
    rows[...] = jnp.zeros(rows.shape, jnp.float32)
    rows[:, :width] = jnp.broadcast_to(enthalpy[...].reshape(1, width), (cells, width))
    formation[...] = rows[...].T
    rows[...] = jnp.zeros(rows.shape, jnp.float32)
    factors[...] = jnp.broadcast_to(rate_factor[...].reshape(1, depth), (cells, depth)).T
    spread = diffusivity[...].reshape(1, width)

    def turn_weights():
        loads[0].wait()
        whole = width // 128 * 128
        for first in range(0, whole, 128):
            weights_turned[:, first : first + 128] = weights_in[first : first + 128, :].T
        if whole < width:
            weights_tail[...] = jnp.zeros(weights_tail.shape, jnp.float32)
            weights_tail[: width - whole, :] = weights_in[whole:, :].astype(jnp.float32)
            weights_turned[:, whole : whole + 128] = weights_tail[...].T.astype(jnp.bfloat16)
        if whole + 128 < padded:
            weights_turned[:, whole + 128 :] = jnp.zeros(
                (depth, padded - whole - 128), jnp.bfloat16
            )

    turn_weights()

    def section(phase):
        block = species if phase == 0 else middle
        for x in range(cx):
            low_x = halo_x[phase, 0] if x == 0 else block[x - 1]
            high_x = halo_x[phase, 1] if x == cx - 1 else block[x + 1]
            for y in range(cy):
                now = block[x, y]
                low_y = halo_y[phase, 0, x] if y == 0 else block[x, y - 1]
                high_y = halo_y[phase, 1, x] if y == cy - 1 else block[x, y + 1]
                low_z = jnp.concatenate([halo_z[phase, 0, x, y], now[: cz - 1]], axis=0)
                high_z = jnp.concatenate([now[1:], halo_z[phase, 1, x, y]], axis=0)
                beside = low_x[y] + high_x[y] + low_y + high_y + low_z + high_z
                result = now + cell_scale[y][:, x : x + 1] * spread * (beside - 6.0 * now)
                if phase == 0:
                    middle[x, y] = result
                else:
                    first = x * cy * cz + y * cz
                    rows[first : first + cz, :width] = result

    each_face(lambda axis_no, side: face_copy(0, axis_no, side, side).wait_recv())
    section(0)
    fill_face_z(1)
    each_face(lambda axis_no, side: face_copy(1, axis_no, side, 1 - side).start())
    each_face(lambda axis_no, side: face_copy(1, axis_no, side, side).wait_recv())
    section(1)

    loads[1].wait()
    state[...] = rows[...].T
    start_state[...] = state[...]
    chunk = 256 if depth % 256 == 0 else depth

    def substep(step, carried):
        rounded = state[...].astype(jnp.bfloat16)
        for first in range(0, depth, chunk):
            activity = jnp.dot(
                weights_turned[first : first + chunk, :],
                rounded,
                preferred_element_type=jnp.float32,
            )
            soft = jnp.maximum(activity, 0.0) + jnp.log(1.0 + jnp.exp(-jnp.abs(activity)))
            rates[first : first + chunk, :] = (
                factors[first : first + chunk, :] * soft
            ).astype(jnp.bfloat16)
        change = jnp.dot(weights_out[...], rates[...], preferred_element_type=jnp.float32)
        now = state[:width, :]
        active = cell_counts[...] > step.astype(jnp.float32)
        state[:width, :] = jnp.where(active, now + relax_rate * (change - now), now)
        return carried

    lax.fori_loop(0, MAXSUB, substep, 0)

    released = jnp.sum(
        formation[...] * (start_state[...] - state[...]), axis=0, keepdims=True
    )
    for worker in range(group):
        heat_part[worker] = jnp.where(cell_targets[...] == jnp.float32(worker), released, 0.0)

    def heat_copy(offset):
        return pltpu.make_async_remote_copy(
            src_ref=heat_part.at[lax.rem(me + offset, group)],
            dst_ref=heat_all.at[offset],
            send_sem=heat_send.at[offset],
            recv_sem=heat_recv.at[offset],
            device_id=peer(offset),
            device_id_type=MESH,
        )

    for offset in range(1, group):
        heat_copy(offset).start()

    rows[...] = state[...].T
    for x in range(cx):
        for y in range(cy):
            first = x * cy * cz + y * cz
            advanced[x, y] = rows[first : first + cz, :width]

    total = heat_part[me]
    for offset in range(1, group):
        heat_copy(offset).wait_recv()
        total = total + heat_all[offset]
    worker_heat[0] = jnp.sum(total, axis=1, keepdims=True) / cells

    for phase in range(2):
        each_face(
            lambda axis_no, side, phase=phase: face_copy(
                phase, axis_no, side, 1 - side
            ).wait_send()
        )
    for offset in range(1, group):
        heat_copy(offset).wait_send()


def local(
    species,
    counts,
    assignment,
    cell_scale,
    diffusivity,
    order_weights,
    stoichiometry,
    rate_factor,
    enthalpy,
):
    group = lax.axis_size("gx") * lax.axis_size("gy")
    cx, cy, cz, width = species.shape
    cells = cx * cy * cz
    depth = order_weights.shape[1]
    padded = -(-width // 256) * 256
    vmem = pl.BlockSpec(memory_space=pltpu.VMEM)
    hbm = pl.BlockSpec(memory_space=pltpu.HBM)
    single = jnp.float32
    flops = 4 * MAXSUB * cells * width * depth
    return pl.pallas_call(
        kernel,
        out_shape=(
            jax.ShapeDtypeStruct(species.shape, single),
            jax.ShapeDtypeStruct((1, 1, 1), single),
        ),
        in_specs=[vmem, vmem, vmem, vmem, vmem, hbm, hbm, vmem, vmem],
        out_specs=(vmem, vmem),
        scratch_shapes=[
            pltpu.VMEM(order_weights.shape, jnp.bfloat16),
            pltpu.VMEM(stoichiometry.shape[::-1], jnp.bfloat16),
            pltpu.VMEM((128, depth), single),
            pltpu.VMEM((depth, padded), jnp.bfloat16),
            pltpu.VMEM((2, 2, cy, cz, width), single),
            pltpu.VMEM((2, 2, cx, cz, width), single),
            pltpu.VMEM((2, 2, cx, cy, 1, width), single),
            pltpu.VMEM((2, 2, cx, cy, 1, width), single),
            pltpu.VMEM(species.shape, single),
            pltpu.VMEM((cells, padded), single),
            pltpu.VMEM((padded, cells), single),
            pltpu.VMEM((padded, cells), single),
            pltpu.VMEM((depth, cells), jnp.bfloat16),
            pltpu.VMEM((depth, cells), single),
            pltpu.VMEM((padded, cells), single),
            pltpu.VMEM((1, cells), single),
            pltpu.VMEM((1, cells), single),
            pltpu.VMEM((group, 1, cells), single),
            pltpu.VMEM((group, 1, cells), single),
            pltpu.SemaphoreType.DMA((2,)),
            pltpu.SemaphoreType.DMA((2, 3, 2)),
            pltpu.SemaphoreType.DMA((2, 3, 2)),
            pltpu.SemaphoreType.DMA((group,)),
            pltpu.SemaphoreType.DMA((group,)),
        ],
        compiler_params=pltpu.CompilerParams(
            collective_id=0, has_side_effects=True, vmem_limit_bytes=48 * 1024 * 1024
        ),
        cost_estimate=pl.CostEstimate(
            flops=flops, bytes_accessed=5_000_000, transcendentals=2 * MAXSUB * cells * depth
        ),
    )(
        species,
        counts.transpose(1, 2, 0),
        assignment.transpose(1, 2, 0),
        cell_scale.transpose(1, 2, 0),
        diffusivity,
        order_weights,
        stoichiometry.T,
        rate_factor,
        enthalpy,
    )


def solution(mesh):
    placed = (
        P("gx", "gy", "gz", None),
        P("gx", "gy", "gz"),
        P("gx", "gy", "gz"),
        P("gx", "gy", "gz"),
        P(),
        P(),
        P(),
        P(),
        P(),
    )
    return jax.shard_map(
        local,
        mesh=mesh,
        in_specs=placed,
        out_specs=(P("gx", "gy", "gz", None), P("gx", "gy", "gz")),
        check_vma=False,
    )
```

time: 106 us -> 40.6 us (0.38)
  starting transfers between devices: 33.5 us -> 0 us
  Pallas kernels: 0 us -> 28.7 us
  matrix products: 24.3 us -> 0 us
  blocking collectives: 13.5 us -> 0 us
  waiting for transfers between devices: 8.59 us -> 0 us
  between operations: 8.09 us -> 2.41 us
  other arithmetic: 4.69 us -> 0 us
  local copies, waits for them, and re-layouts: 11.5 us -> 9.02 us
    ppermute x12 -> x0, starting transfers between devices: 33.5 us -> none  [the longest x6 25.8 us: extended(): lax.ppermute(lax.slice_in_dim(block, block.shape[dim] - width, None, axis...]
    pallas_call x0 -> x1, Pallas kernels: none -> 28.7 us  [local(): pl.pallas_call(kernel, out_shape=(jax.ShapeDtypeStruct(species.shape, sin...]
    dot_general x8 -> x0, matrix products: 24.3 us -> none  [substep(): jnp.dot(rate_values, stoichiometry, preferred_element_type=jnp.float32)]
    unnamed x1 -> x0, blocking collectives: 13.5 us -> none
    ppermute x12 -> x0, waiting for transfers between devices: 8.59 us -> none  [the longest x6 4.5 us: extended(): lax.ppermute(lax.slice_in_dim(block, 0, width, axis=dim), axis, backward)]
    unnamed x19, local copies, waits for them, and re-layouts: 4.44 us -> 9.02 us
    gather x4 -> x0, local copies, waits for them, and re-layouts: 4.09 us -> none  [the longest x2 2.04 us: advance(): return (sorted_rows[inverse], heat_rows[inverse])]
    sort x1 -> x0, other arithmetic: 2.54 us -> none  [advance(): ordering = jnp.argsort(scores, stable=True)]
  transfers between devices with their start and end apart: 12 -> 0, of which waited for: 5 -> 0; matrix products, arithmetic and copies ran while one was open for 7% -> 0% of each run, Pallas kernels for 0% -> 0%
where the time goes in v1:
time: 40.6 us; the launch traced here: 40.1 us
  Pallas kernels  28.7 us (71%)
  local copies, waits for them, and re-layouts  9.02 us (22%)
  between operations  2.41 us (6%)
    pallas_call x1, Pallas kernels, local(): pl.pallas_call(kernel, out_shape=(jax.ShapeDtypeStruct(species.shape, sin...  28.7 us
    unnamed x19, local copies, waits for them, and re-layouts  9.02 us

profile of v1, /device:TPU:0, one launch (start us, length us, event | category | flops | bytes accessed | tf_op | source)
XLA Modules:
  0.0 40.1 jit_solution(463467808510967475)
XLA Ops:
  0.6 0.0 copy-start
  0.6 1.6 %copy-done = bf16[654,1536]{1,0:T(8,128)(2,1)S(1)} copy-done((bf16[654,1536]{1,0:T(8,128)(2,1)S(1)}, bf16[654,1536]{1,0:T(8,128)(2,1)}, u32[]{:S(2)}) %copy-start) | copy-done | bytes 2009112
  2.2 0.0 copy-start.1
  2.2 1.6 %copy-done.1 = bf16[1536,654]{0,1:T(8,128)(2,1)S(1)} copy-done((bf16[1536,654]{0,1:T(8,128)(2,1)S(1)}, bf16[1536,654]{0,1:T(8,128)(2,1)}, u32[]{:S(2)}) %copy-start.1) | copy-done | bytes 2009112
  3.8 0.0 copy-start.2
  3.8 1.0 %copy-done.2 = f32[8,4,4,654]{3,2,1,0:T(4,128)S(1)} copy-done((f32[8,4,4,654]{3,2,1,0:T(4,128)S(1)}, f32[8,4,4,654]{3,2,1,0:T(4,128)}, u32[]{:S(2)}) %copy-start.2) | copy-done | bytes 334872
  4.8 0.0 copy-start.3
  4.8 0.7 %copy-done.3 = s32[8,4,4]{0,2,1:T(4,128)S(1)} copy-done((s32[8,4,4]{0,2,1:T(4,128)S(1)}, s32[8,4,4]{0,2,1:T(4,128)}, u32[]{:S(2)}) %copy-start.3) | copy-done | bytes 536
  5.5 0.0 copy-start.4
  5.5 0.7 %copy-done.4 = s32[8,4,4]{0,2,1:T(4,128)S(1)} copy-done((s32[8,4,4]{0,2,1:T(4,128)S(1)}, s32[8,4,4]{0,2,1:T(4,128)}, u32[]{:S(2)}) %copy-start.4) | copy-done | bytes 536
  6.1 0.0 copy-start.5
  6.2 0.7 %copy-done.5 = f32[8,4,4]{0,2,1:T(4,128)S(1)} copy-done((f32[8,4,4]{0,2,1:T(4,128)S(1)}, f32[8,4,4]{0,2,1:T(4,128)}, u32[]{:S(2)}) %copy-start.5) | copy-done | bytes 536
  6.8 0.0 copy-start.6
  6.8 0.7 %copy-done.6 = f32[1536]{0:T(1024)S(1)} copy-done((f32[1536]{0:T(1024)S(1)}, f32[1536]{0:T(1024)}, u32[]{:S(2)}) %copy-start.6) | copy-done | bytes 6168
  7.5 0.0 copy-start.7
  7.5 0.7 %copy-done.7 = f32[654]{0:T(1024)S(1)} copy-done((f32[654]{0:T(1024)S(1)}, f32[654]{0:T(1024)}, u32[]{:S(2)}) %copy-start.7) | copy-done | bytes 2640
  8.2 0.0 copy-start.8
  8.2 0.7 %copy-done.8 = f32[654]{0:T(1024)S(1)} copy-done((f32[654]{0:T(1024)S(1)}, f32[654]{0:T(1024)}, u32[]{:S(2)}) %copy-start.8) | copy-done | bytes 2640
  8.9 28.7 %shard_map.104 = (f32[8,4,4,654]{3,2,1,0:T(4,128)S(1)}, f32[1,1,1]{2,1,0:T(1,128)}) custom-call(f32[8,4,4,654]{3,2,1,0:T(4,128)S(1)} %copy-done.2, s32[4,4,8]{2,1,0:T(4,128)S(1)} %bitcast.5, s32[4,4,8]{2,1,0:T(4,128)S(1)} %bitcast.6, f32[4,4,8]{2,1,0:T(4,128)S(1)} %bitcast.7, f32[654]{0:T(1024)S(1)} %copy-done.7, bf16[654,1536]{1,0:T(8,128)(2,1)S(1)} %copy-done, ...), custom_call_target="tpu_custom_call" | custom-call | flops 4114612224 | bytes 5000000 | tf_op jit(solution)/shard_map/pallas_call | solution.py:276
  37.6 0.7 %copy.13 = f32[8,4,4,654]{3,2,1,0:T(4,128)} copy(f32[8,4,4,654]{3,2,1,0:T(4,128)S(1)} %get-tuple-element.4) | data formatting | bytes 669696
Async XLA Ops:
  0.6 1.6 %copy-start = (bf16[654,1536]{1,0:T(8,128)(2,1)S(1)}, bf16[654,1536]{1,0:T(8,128)(2,1)}, u32[]{:S(2)}) copy-start(bf16[654,1536]{1,0:T(8,128)(2,1)} %order_weights.1) | copy-start | bytes 6027268
  2.2 1.6 %copy-start.1 = (bf16[1536,654]{0,1:T(8,128)(2,1)S(1)}, bf16[1536,654]{0,1:T(8,128)(2,1)}, u32[]{:S(2)}) copy-start(bf16[1536,654]{0,1:T(8,128)(2,1)} %param.15) | copy-start | bytes 6027268
  3.8 1.0 %copy-start.2 = (f32[8,4,4,654]{3,2,1,0:T(4,128)S(1)}, f32[8,4,4,654]{3,2,1,0:T(4,128)}, u32[]{:S(2)}) copy-start(f32[8,4,4,654]{3,2,1,0:T(4,128)} %species.1) | copy-start | bytes 1004548
  4.8 0.7 %copy-start.3 = (s32[8,4,4]{0,2,1:T(4,128)S(1)}, s32[8,4,4]{0,2,1:T(4,128)}, u32[]{:S(2)}) copy-start(s32[8,4,4]{0,2,1:T(4,128)} %param.10) | copy-start | bytes 1540
  5.5 0.7 %copy-start.4 = (s32[8,4,4]{0,2,1:T(4,128)S(1)}, s32[8,4,4]{0,2,1:T(4,128)}, u32[]{:S(2)}) copy-start(s32[8,4,4]{0,2,1:T(4,128)} %param.11) | copy-start | bytes 1540
  6.1 0.7 %copy-start.5 = (f32[8,4,4]{0,2,1:T(4,128)S(1)}, f32[8,4,4]{0,2,1:T(4,128)}, u32[]{:S(2)}) copy-start(f32[8,4,4]{0,2,1:T(4,128)} %param.12) | copy-start | bytes 1540
  6.8 0.7 %copy-start.6 = (f32[1536]{0:T(1024)S(1)}, f32[1536]{0:T(1024)}, u32[]{:S(2)}) copy-start(f32[1536]{0:T(1024)} %rate_factor.1) | copy-start | bytes 18436
  7.5 0.7 %copy-start.7 = (f32[654]{0:T(1024)S(1)}, f32[654]{0:T(1024)}, u32[]{:S(2)}) copy-start(f32[654]{0:T(1024)} %diffusivity.1) | copy-start | bytes 7852
  8.2 0.7 %copy-start.8 = (f32[654]{0:T(1024)S(1)}, f32[654]{0:T(1024)}, u32[]{:S(2)}) copy-start(f32[654]{0:T(1024)} %enthalpy.1) | copy-start | bytes 7852

commit v2 on v1

--- a/solution.py
+++ b/solution.py
@@ -11,43 +11,38 @@
 MESH = pl.DeviceIdType.MESH
 
 
-def kernel(
-    species,
-    counts,
-    assignment,
-    cell_scale,
-    diffusivity,
-    order_weights,
-    stoichiometry,
-    rate_factor,
-    enthalpy,
-    advanced,
-    worker_heat,
-    weights_in,
-    weights_out,
-    weights_tail,
-    weights_turned,
-    halo_x,
-    halo_y,
-    halo_z,
-    face_z,
-    middle,
-    rows,
-    start_state,
-    state,
-    rates,
-    factors,
-    formation,
-    cell_counts,
-    cell_targets,
-    heat_part,
-    heat_all,
-    load_sem,
-    send_sem,
-    recv_sem,
-    heat_send,
-    heat_recv,
-):
+def kernel(*refs):
+    operands, refs = refs[:9], refs[9:]
+    (
+        advanced,
+        worker_heat,
+        *held,
+        weights_in,
+        weights_out,
+        weights_tail,
+        weights_turned,
+        halo_x,
+        halo_y,
+        halo_z,
+        face_z,
+        middle,
+        rows,
+        start_state,
+        state,
+        rates,
+        factors,
+        formation,
+        cell_counts,
+        cell_targets,
+        heat_part,
+        heat_all,
+        load_sem,
+        send_sem,
+        recv_sem,
+        heat_send,
+        heat_recv,
+    ) = refs
+    species, counts, assignment, cell_scale, diffusivity, rate_factor, enthalpy = held
     spans = [lax.axis_size(axis) for axis in AXES]
     here = [lax.axis_index(axis) for axis in AXES]
     span_y = spans[1]
@@ -55,14 +50,16 @@
     me = here[0] * span_y + here[1]
     cx, cy, cz, width = species.shape
     cells = cx * cy * cz
-    depth = order_weights.shape[1]
-
+    depth = weights_in.shape[1]
+
+    places = (species, counts, assignment, cell_scale, diffusivity, weights_in, weights_out)
+    places = places + (rate_factor, enthalpy)
     loads = [
-        pltpu.make_async_copy(order_weights, weights_in, load_sem.at[0]),
-        pltpu.make_async_copy(stoichiometry, weights_out, load_sem.at[1]),
+        pltpu.make_async_copy(operand, place, load_sem.at[number])
+        for number, (operand, place) in enumerate(zip(operands, places))
     ]
-    for load in loads:
-        load.start()
+    for number in (0, 1, 2, 3, 4, 5, 7, 8, 6):
+        loads[number].start()
 
     def present(axis_no, side):
         if side == 0:
@@ -101,20 +98,14 @@
             device_id_type=MESH,
         )
 
-    def fill_face_z(phase):
-        block = species if phase == 0 else middle
-        face_z[phase, 0] = block[:, :, 0:1, :]
-        face_z[phase, 1] = block[:, :, cz - 1 : cz, :]
-
-    def each_face(action):
-        for axis_no in (2, 1, 0):
+    def each_face(action, axes=(2, 1, 0)):
+        for axis_no in axes:
             for side in range(2):
 
                 @pl.when(present(axis_no, side))
                 def _(axis_no=axis_no, side=side):
                     action(axis_no, side)
 
-    fill_face_z(0)
     for phase in range(2):
         for side in range(2):
             for axis_no, halo in enumerate((halo_x, halo_y, halo_z)):
@@ -127,9 +118,17 @@
         barrier,
         group - 1 + present(2, 0).astype(jnp.int32) + present(2, 1).astype(jnp.int32),
     )
-    each_face(lambda axis_no, side: face_copy(0, axis_no, side, 1 - side).start())
-
+    loads[0].wait()
+    for axes in ((1, 0), (2,)):
+        if axes == (2,):
+            face_z[0, 0] = species[:, :, 0:1, :]
+            face_z[0, 1] = species[:, :, cz - 1 : cz, :]
+        each_face(lambda axis_no, side: face_copy(0, axis_no, side, 1 - side).start(), axes)
+
+    padded = rows.shape[1]
     rows[...] = jnp.zeros(rows.shape, jnp.float32)
+    for number in range(1, 5):
+        loads[number].wait()
     for source, target in ((counts, cell_counts), (assignment, cell_targets)):
         for x in range(cx):
             for y in range(cy):
@@ -137,19 +136,15 @@
                 column = source[y][:, x : x + 1].astype(jnp.float32)
                 rows[first : first + cz, :cells] = jnp.broadcast_to(column, (cz, cells))
         target[...] = rows[:, :cells].T[:1]
-    padded = rows.shape[1]
-    rows[...] = jnp.zeros(rows.shape, jnp.float32)
-    rows[:, :width] = jnp.broadcast_to(enthalpy[...].reshape(1, width), (cells, width))
-    formation[...] = rows[...].T
-    rows[...] = jnp.zeros(rows.shape, jnp.float32)
-    factors[...] = jnp.broadcast_to(rate_factor[...].reshape(1, depth), (cells, depth)).T
     spread = diffusivity[...].reshape(1, width)
 
-    def turn_weights():
-        loads[0].wait()
-        whole = width // 128 * 128
-        for first in range(0, whole, 128):
+    whole = width // 128 * 128
+
+    def turn_weights(begin, end):
+        for first in range(begin, end, 128):
             weights_turned[:, first : first + 128] = weights_in[first : first + 128, :].T
+
+    def turn_tail():
         if whole < width:
             weights_tail[...] = jnp.zeros(weights_tail.shape, jnp.float32)
             weights_tail[: width - whole, :] = weights_in[whole:, :].astype(jnp.float32)
@@ -159,51 +154,74 @@
                 (depth, padded - whole - 128), jnp.bfloat16
             )
 
-    turn_weights()
-
-    def section(phase):
+    def section(phase, places):
         block = species if phase == 0 else middle
-        for x in range(cx):
-            low_x = halo_x[phase, 0] if x == 0 else block[x - 1]
-            high_x = halo_x[phase, 1] if x == cx - 1 else block[x + 1]
-            for y in range(cy):
-                now = block[x, y]
-                low_y = halo_y[phase, 0, x] if y == 0 else block[x, y - 1]
-                high_y = halo_y[phase, 1, x] if y == cy - 1 else block[x, y + 1]
-                low_z = jnp.concatenate([halo_z[phase, 0, x, y], now[: cz - 1]], axis=0)
-                high_z = jnp.concatenate([now[1:], halo_z[phase, 1, x, y]], axis=0)
-                beside = low_x[y] + high_x[y] + low_y + high_y + low_z + high_z
-                result = now + cell_scale[y][:, x : x + 1] * spread * (beside - 6.0 * now)
-                if phase == 0:
-                    middle[x, y] = result
-                else:
-                    first = x * cy * cz + y * cz
-                    rows[first : first + cz, :width] = result
-
+        for x, y in places:
+            low_x = halo_x[phase, 0, y] if x == 0 else block[x - 1, y]
+            high_x = halo_x[phase, 1, y] if x == cx - 1 else block[x + 1, y]
+            now = block[x, y]
+            low_y = halo_y[phase, 0, x] if y == 0 else block[x, y - 1]
+            high_y = halo_y[phase, 1, x] if y == cy - 1 else block[x, y + 1]
+            low_z = jnp.concatenate([halo_z[phase, 0, x, y], now[: cz - 1]], axis=0)
+            high_z = jnp.concatenate([now[1:], halo_z[phase, 1, x, y]], axis=0)
+            beside = low_x + high_x + low_y + high_y + low_z + high_z
+            scale = cell_scale[y][:, x : x + 1]
+            result = now + scale * spread * (beside - 6.0 * now)
+            if phase == 0:
+                middle[x, y] = result
+                face_z[1, 0, x, y] = result[:1]
+                face_z[1, 1, x, y] = result[cz - 1 :]
+            else:
+                first = x * cy * cz + y * cz
+                rows[first : first + cz, :width] = result
+
+    everywhere = [(x, y) for x in range(cx) for y in range(cy)]
+    order = [[], [], []]
+    for x, y in everywhere:
+        order[0 if x in (0, cx - 1) else 1 if y in (0, cy - 1) else 2].append((x, y))
+
+    halfway = whole // 256 * 128
+    loads[5].wait()
+    turn_weights(0, halfway)
     each_face(lambda axis_no, side: face_copy(0, axis_no, side, side).wait_recv())
-    section(0)
-    fill_face_z(1)
-    each_face(lambda axis_no, side: face_copy(1, axis_no, side, 1 - side).start())
+    for axis_no in range(3):
+        section(0, order[axis_no])
+        each_face(
+            lambda axis_no, side: face_copy(1, axis_no, side, 1 - side).start(), (axis_no,)
+        )
+    turn_weights(halfway, whole)
+    turn_tail()
+    for number in (7, 8):
+        loads[number].wait()
+    rows[:, :width] = jnp.broadcast_to(enthalpy[...].reshape(1, width), (cells, width))
+    formation[...] = rows[...].T
+    factors[...] = jnp.broadcast_to(rate_factor[...].reshape(1, depth), (cells, depth)).T
     each_face(lambda axis_no, side: face_copy(1, axis_no, side, side).wait_recv())
-    section(1)
-
-    loads[1].wait()
+    section(1, everywhere)
+
+    loads[6].wait()
     state[...] = rows[...].T
     start_state[...] = state[...]
     chunk = 256 if depth % 256 == 0 else depth
 
     def substep(step, carried):
         rounded = state[...].astype(jnp.bfloat16)
-        for first in range(0, depth, chunk):
-            activity = jnp.dot(
+
+        def activities(first):
+            return jnp.dot(
                 weights_turned[first : first + chunk, :],
                 rounded,
                 preferred_element_type=jnp.float32,
             )
+
+        activity = activities(0)
+        for first in range(0, depth, chunk):
+            later = activities(first + chunk) if first + chunk < depth else None
             soft = jnp.maximum(activity, 0.0) + jnp.log(1.0 + jnp.exp(-jnp.abs(activity)))
             rates[first : first + chunk, :] = (
                 factors[first : first + chunk, :] * soft
             ).astype(jnp.bfloat16)
+            activity = later
         change = jnp.dot(weights_out[...], rates[...], preferred_element_type=jnp.float32)
         now = state[:width, :]
         active = cell_counts[...] > step.astype(jnp.float32)
@@ -270,7 +288,7 @@
     depth = order_weights.shape[1]
     padded = -(-width // 256) * 256
     vmem = pl.BlockSpec(memory_space=pltpu.VMEM)
-    hbm = pl.BlockSpec(memory_space=pltpu.HBM)
+    hbm = pl.BlockSpec(memory_space=pl.ANY)
     single = jnp.float32
     flops = 4 * MAXSUB * cells * width * depth
     return pl.pallas_call(
@@ -279,9 +297,16 @@
             jax.ShapeDtypeStruct(species.shape, single),
             jax.ShapeDtypeStruct((1, 1, 1), single),
         ),
-        in_specs=[vmem, vmem, vmem, vmem, vmem, hbm, hbm, vmem, vmem],
+        in_specs=[hbm] * 9,
         out_specs=(vmem, vmem),
         scratch_shapes=[
+            pltpu.VMEM(species.shape, single),
+            pltpu.VMEM((cy, cz, cx), counts.dtype),
+            pltpu.VMEM((cy, cz, cx), assignment.dtype),
+            pltpu.VMEM((cy, cz, cx), single),
+            pltpu.VMEM(diffusivity.shape, single),
+            pltpu.VMEM(rate_factor.shape, single),
+            pltpu.VMEM(enthalpy.shape, single),
             pltpu.VMEM(order_weights.shape, jnp.bfloat16),
             pltpu.VMEM(stoichiometry.shape[::-1], jnp.bfloat16),
             pltpu.VMEM((128, depth), single),
@@ -301,14 +326,14 @@
             pltpu.VMEM((1, cells), single),
             pltpu.VMEM((group, 1, cells), single),
             pltpu.VMEM((group, 1, cells), single),
-            pltpu.SemaphoreType.DMA((2,)),
+            pltpu.SemaphoreType.DMA((9,)),
             pltpu.SemaphoreType.DMA((2, 3, 2)),
             pltpu.SemaphoreType.DMA((2, 3, 2)),
             pltpu.SemaphoreType.DMA((group,)),
             pltpu.SemaphoreType.DMA((group,)),
         ],
         compiler_params=pltpu.CompilerParams(
-            collective_id=0, has_side_effects=True, vmem_limit_bytes=48 * 1024 * 1024
+            collective_id=0, has_side_effects=True, vmem_limit_bytes=63 * 1024 * 1024
         ),
         cost_estimate=pl.CostEstimate(
             flops=flops, bytes_accessed=5_000_000, transcendentals=2 * MAXSUB * cells * depth

time: 40.6 us -> 32.7 us (0.81)
  local copies, waits for them, and re-layouts: 9.02 us -> 1.77 us
    unnamed x19 -> x1, local copies, waits for them, and re-layouts: 9.02 us -> 1.77 us
where the time goes in v2:
time: 32.7 us; the launch traced here: 32.5 us
  Pallas kernels  28.4 us (87%)
  between operations  2.39 us (7%)
  local copies, waits for them, and re-layouts  1.77 us (5%)
    pallas_call x1, Pallas kernels, local(): pl.pallas_call(kernel, out_shape=(jax.ShapeDtypeStruct(species.shape, sin...  28.4 us
    unnamed x1, local copies, waits for them, and re-layouts  1.77 us

profile of v2, /device:TPU:0, one launch (start us, length us, event | category | flops | bytes accessed | tf_op | source)
XLA Modules:
  0.0 32.5 jit_solution(3897355104443932779)
XLA Ops:
  0.6 28.4 %shard_map.104 = (f32[8,4,4,654]{3,2,1,0:T(4,128)}, f32[1,1,1]{2,1,0:T(1,128)}) custom-call(f32[8,4,4,654]{3,2,1,0:T(4,128)} %refs_0_.1, s32[4,4,8]{2,1,0:T(4,128)} %bitcast.5, s32[4,4,8]{2,1,0:T(4,128)} %bitcast.6, f32[4,4,8]{2,1,0:T(4,128)} %bitcast.7, f32[654]{0:T(1024)} %refs_4_.1, bf16[654,1536]{1,0:T(8,128)(2,1)} %refs_5_.1, ...), custom_call_target="tpu_custom_call" | custom-call | flops 4114612224 | bytes 5000000 | tf_op jit(solution)/shard_map/pallas_call | solution.py:294
  29.0 1.8 %copy.13 = f32[8,4,4,654]{3,2,1,0:T(4,128)} copy(f32[8,4,4,654]{3,2,1,0:T(4,128)} %get-tuple-element.4) | data formatting | bytes 669696

commit v3 on v2

--- a/solution.py
+++ b/solution.py
@@ -27,11 +27,8 @@
         face_z,
         middle,
         rows,
-        start_state,
-        state,
-        rates,
-        factors,
-        formation,
+        start_rows,
+        staged,
         cell_counts,
         cell_targets,
         heat_part,
@@ -58,7 +55,7 @@
         pltpu.make_async_copy(operand, place, load_sem.at[number])
         for number, (operand, place) in enumerate(zip(operands, places))
     ]
-    for number in (0, 1, 2, 3, 4, 5, 7, 8, 6):
+    for number in (0, 1, 2, 3, 4, 6, 5, 7, 8):
         loads[number].start()
 
     def present(axis_no, side):
@@ -114,16 +111,14 @@
                 def _(phase=phase, side=side, halo=halo):
                     halo[phase, side] = jnp.zeros(halo.shape[2:], jnp.float32)
 
+    loads[0].wait()
+    face_z[0, 0] = species[:, :, 0:1, :]
+    face_z[0, 1] = species[:, :, cz - 1 : cz, :]
     pl.semaphore_wait(
         barrier,
         group - 1 + present(2, 0).astype(jnp.int32) + present(2, 1).astype(jnp.int32),
     )
-    loads[0].wait()
-    for axes in ((1, 0), (2,)):
-        if axes == (2,):
-            face_z[0, 0] = species[:, :, 0:1, :]
-            face_z[0, 1] = species[:, :, cz - 1 : cz, :]
-        each_face(lambda axis_no, side: face_copy(0, axis_no, side, 1 - side).start(), axes)
+    each_face(lambda axis_no, side: face_copy(0, axis_no, side, 1 - side).start())
 
     padded = rows.shape[1]
     rows[...] = jnp.zeros(rows.shape, jnp.float32)
@@ -134,20 +129,19 @@
             for y in range(cy):
                 first = x * cy * cz + y * cz
                 column = source[y][:, x : x + 1].astype(jnp.float32)
-                rows[first : first + cz, :cells] = jnp.broadcast_to(column, (cz, cells))
-        target[...] = rows[:, :cells].T[:1]
+                target[first : first + cz, :] = jnp.broadcast_to(column, (cz, target.shape[1]))
     spread = diffusivity[...].reshape(1, width)
 
     whole = width // 128 * 128
 
     def turn_weights(begin, end):
         for first in range(begin, end, 128):
-            weights_turned[:, first : first + 128] = weights_in[first : first + 128, :].T
+            weights_turned[:, first : first + 128] = weights_out[first : first + 128, :].T
 
     def turn_tail():
         if whole < width:
             weights_tail[...] = jnp.zeros(weights_tail.shape, jnp.float32)
-            weights_tail[: width - whole, :] = weights_in[whole:, :].astype(jnp.float32)
+            weights_tail[: width - whole, :] = weights_out[whole:, :].astype(jnp.float32)
             weights_turned[:, whole : whole + 128] = weights_tail[...].T.astype(jnp.bfloat16)
         if whole + 128 < padded:
             weights_turned[:, whole + 128 :] = jnp.zeros(
@@ -181,7 +175,7 @@
         order[0 if x in (0, cx - 1) else 1 if y in (0, cy - 1) else 2].append((x, y))
 
     halfway = whole // 256 * 128
-    loads[5].wait()
+    loads[6].wait()
     turn_weights(0, halfway)
     each_face(lambda axis_no, side: face_copy(0, axis_no, side, side).wait_recv())
     for axis_no in range(3):
@@ -191,54 +185,58 @@
         )
     turn_weights(halfway, whole)
     turn_tail()
-    for number in (7, 8):
+    for number in (5, 7, 8):
         loads[number].wait()
-    rows[:, :width] = jnp.broadcast_to(enthalpy[...].reshape(1, width), (cells, width))
-    formation[...] = rows[...].T
-    factors[...] = jnp.broadcast_to(rate_factor[...].reshape(1, depth), (cells, depth)).T
+    factors = rate_factor[...].reshape(1, depth)
     each_face(lambda axis_no, side: face_copy(1, axis_no, side, side).wait_recv())
     section(1, everywhere)
 
-    loads[6].wait()
-    state[...] = rows[...].T
-    start_state[...] = state[...]
+    start_rows[...] = rows[...]
     chunk = 256 if depth % 256 == 0 else depth
 
     def substep(step, carried):
-        rounded = state[...].astype(jnp.bfloat16)
+        rounded = rows[:, :width].astype(jnp.bfloat16)
 
         def activities(first):
             return jnp.dot(
-                weights_turned[first : first + chunk, :],
                 rounded,
+                weights_in[:, first : first + chunk],
                 preferred_element_type=jnp.float32,
             )
 
+        change = jnp.zeros((cells, padded), jnp.float32)
         activity = activities(0)
         for first in range(0, depth, chunk):
             later = activities(first + chunk) if first + chunk < depth else None
             soft = jnp.maximum(activity, 0.0) + jnp.log(1.0 + jnp.exp(-jnp.abs(activity)))
-            rates[first : first + chunk, :] = (
-                factors[first : first + chunk, :] * soft
-            ).astype(jnp.bfloat16)
+            rate_values = (factors[:, first : first + chunk] * soft).astype(jnp.bfloat16)
+            change = change + jnp.dot(
+                rate_values,
+                weights_turned[first : first + chunk, :],
+                preferred_element_type=jnp.float32,
+            )
             activity = later
-        change = jnp.dot(weights_out[...], rates[...], preferred_element_type=jnp.float32)
-        now = state[:width, :]
-        active = cell_counts[...] > step.astype(jnp.float32)
-        state[:width, :] = jnp.where(active, now + relax_rate * (change - now), now)
+        now = rows[...]
+        active = cell_counts[:, 0:1] > step.astype(jnp.float32)
+        rows[...] = jnp.where(active, now + relax_rate * (change - now), now)
         return carried
 
     lax.fori_loop(0, MAXSUB, substep, 0)
 
     released = jnp.sum(
-        formation[...] * (start_state[...] - state[...]), axis=0, keepdims=True
-    )
-    for worker in range(group):
-        heat_part[worker] = jnp.where(cell_targets[...] == jnp.float32(worker), released, 0.0)
+        enthalpy[...].reshape(1, width) * (start_rows[:, :width] - rows[:, :width]),
+        axis=1,
+        keepdims=True,
+    )
+    lanes = heat_part.shape[1]
+    worker = lax.broadcasted_iota(jnp.int32, (cells, lanes), 1).astype(jnp.float32)
+    heat_part[...] = jnp.sum(
+        jnp.where(cell_targets[...] == worker, released, 0.0), axis=0, keepdims=True
+    )
 
     def heat_copy(offset):
         return pltpu.make_async_remote_copy(
-            src_ref=heat_part.at[lax.rem(me + offset, group)],
+            src_ref=heat_part,
             dst_ref=heat_all.at[offset],
             send_sem=heat_send.at[offset],
             recv_sem=heat_recv.at[offset],
@@ -249,17 +247,20 @@
     for offset in range(1, group):
         heat_copy(offset).start()
 
-    rows[...] = state[...].T
     for x in range(cx):
         for y in range(cy):
             first = x * cy * cz + y * cz
-            advanced[x, y] = rows[first : first + cz, :width]
-
-    total = heat_part[me]
+            staged[x, y] = rows[first : first + cz, :width]
+    leave = pltpu.make_async_copy(staged, advanced, load_sem.at[9])
+    leave.start()
+
+    total = heat_part[...]
     for offset in range(1, group):
         heat_copy(offset).wait_recv()
         total = total + heat_all[offset]
-    worker_heat[0] = jnp.sum(total, axis=1, keepdims=True) / cells
+    mine = lax.broadcasted_iota(jnp.int32, (1, lanes), 1) == me
+    worker_heat[0] = jnp.sum(jnp.where(mine, total, 0.0), axis=1, keepdims=True) / cells
+    leave.wait()
 
     for phase in range(2):
         each_face(
@@ -269,6 +270,16 @@
         )
     for offset in range(1, group):
         heat_copy(offset).wait_send()
+
+
+def hand_on(block, result, done):
+    copies = [
+        pltpu.make_async_copy(block.at[x], result.at[x], done.at[x]) for x in range(block.shape[0])
+    ]
+    for copy in copies:
+        copy.start()
+    for copy in copies:
+        copy.wait()
 
 
 def local(
@@ -287,18 +298,19 @@
     cells = cx * cy * cz
     depth = order_weights.shape[1]
     padded = -(-width // 256) * 256
+    lanes = -(-group // 128) * 128
     vmem = pl.BlockSpec(memory_space=pltpu.VMEM)
     hbm = pl.BlockSpec(memory_space=pl.ANY)
     single = jnp.float32
     flops = 4 * MAXSUB * cells * width * depth
-    return pl.pallas_call(
+    advanced, worker_heat = pl.pallas_call(
         kernel,
         out_shape=(
             jax.ShapeDtypeStruct(species.shape, single),
             jax.ShapeDtypeStruct((1, 1, 1), single),
         ),
         in_specs=[hbm] * 9,
-        out_specs=(vmem, vmem),
+        out_specs=(hbm, vmem),
         scratch_shapes=[
             pltpu.VMEM(species.shape, single),
             pltpu.VMEM((cy, cz, cx), counts.dtype),
@@ -317,16 +329,13 @@
             pltpu.VMEM((2, 2, cx, cy, 1, width), single),
             pltpu.VMEM(species.shape, single),
             pltpu.VMEM((cells, padded), single),
-            pltpu.VMEM((padded, cells), single),
-            pltpu.VMEM((padded, cells), single),
-            pltpu.VMEM((depth, cells), jnp.bfloat16),
-            pltpu.VMEM((depth, cells), single),
-            pltpu.VMEM((padded, cells), single),
-            pltpu.VMEM((1, cells), single),
-            pltpu.VMEM((1, cells), single),
-            pltpu.VMEM((group, 1, cells), single),
-            pltpu.VMEM((group, 1, cells), single),
-            pltpu.SemaphoreType.DMA((9,)),
+            pltpu.VMEM((cells, padded), single),
+            pltpu.VMEM(species.shape, single),
+            pltpu.VMEM((cells, lanes), single),
+            pltpu.VMEM((cells, lanes), single),
+            pltpu.VMEM((1, lanes), single),
+            pltpu.VMEM((group, 1, lanes), single),
+            pltpu.SemaphoreType.DMA((10,)),
             pltpu.SemaphoreType.DMA((2, 3, 2)),
             pltpu.SemaphoreType.DMA((2, 3, 2)),
             pltpu.SemaphoreType.DMA((group,)),
@@ -349,6 +358,15 @@
         rate_factor,
         enthalpy,
     )
+    result = pl.pallas_call(
+        hand_on,
+        out_shape=jax.ShapeDtypeStruct(species.shape, single),
+        in_specs=[hbm],
+        out_specs=hbm,
+        scratch_shapes=[pltpu.SemaphoreType.DMA((cx,))],
+        compiler_params=pltpu.CompilerParams(vmem_limit_bytes=63 * 1024 * 1024),
+    )(advanced)
+    return result, worker_heat
 
 
 def solution(mesh):

time: 32.7 us -> 41.4 us (1.27)
  Pallas kernels: 28.4 us -> 38.8 us
  local copies, waits for them, and re-layouts: 1.77 us -> 0 us
    pallas_call x0 -> x1, Pallas kernels: none -> 13.1 us  [local(): pl.pallas_call(hand_on, out_shape=jax.ShapeDtypeStruct(species.shape, sin...]
    pallas_call x1, Pallas kernels: 28.4 us -> 25.8 us  [local(): pl.pallas_call(kernel, out_shape=(jax.ShapeDtypeStruct(species.shape, sin...]
    unnamed x1 -> x0, local copies, waits for them, and re-layouts: 1.77 us -> none
where the time goes in v3:
time: 41.4 us; the launch traced here: 41.2 us
  Pallas kernels  38.8 us (94%)
  between operations  2.4 us (6%)
    pallas_call x1, Pallas kernels, local(): pl.pallas_call(kernel, out_shape=(jax.ShapeDtypeStruct(species.shape, sin...  25.8 us
    pallas_call x1, Pallas kernels, local(): pl.pallas_call(hand_on, out_shape=jax.ShapeDtypeStruct(species.shape, sin...  13.1 us

profile of v3, /device:TPU:0, one launch (start us, length us, event | category | flops | bytes accessed | tf_op | source)
XLA Modules:
  0.0 41.2 jit_solution(4038983062299042404)
XLA Ops:
  0.6 25.8 %shard_map.104 = (f32[8,4,4,654]{3,2,1,0:T(4,128)}, f32[1,1,1]{2,1,0:T(1,128)}) custom-call(f32[8,4,4,654]{3,2,1,0:T(4,128)} %refs_0_.1, s32[4,4,8]{2,1,0:T(4,128)} %bitcast.5, s32[4,4,8]{2,1,0:T(4,128)} %bitcast.6, f32[4,4,8]{2,1,0:T(4,128)} %bitcast.7, f32[654]{0:T(1024)} %refs_4_.1, bf16[654,1536]{1,0:T(8,128)(2,1)} %refs_5_.1, ...), custom_call_target="tpu_custom_call" | custom-call | flops 4114612224 | bytes 5000000 | tf_op jit(solution)/shard_map/pallas_call | solution.py:306
  26.4 13.1 %shard_map.105 = f32[8,4,4,654]{3,2,1,0:T(4,128)} custom-call(f32[8,4,4,654]{3,2,1,0:T(4,128)} %get-tuple-element.4.block), custom_call_target="tpu_custom_call" | custom-call | tf_op jit(solution)/shard_map/pallas_call | solution.py:361

commit v4 on v3

--- a/solution.py
+++ b/solution.py
@@ -28,7 +28,6 @@
         middle,
         rows,
         start_rows,
-        staged,
         cell_counts,
         cell_targets,
         heat_part,
@@ -250,9 +249,7 @@
     for x in range(cx):
         for y in range(cy):
             first = x * cy * cz + y * cz
-            staged[x, y] = rows[first : first + cz, :width]
-    leave = pltpu.make_async_copy(staged, advanced, load_sem.at[9])
-    leave.start()
+            advanced[x, y] = rows[first : first + cz, :width]
 
     total = heat_part[...]
     for offset in range(1, group):
@@ -260,7 +257,6 @@
         total = total + heat_all[offset]
     mine = lax.broadcasted_iota(jnp.int32, (1, lanes), 1) == me
     worker_heat[0] = jnp.sum(jnp.where(mine, total, 0.0), axis=1, keepdims=True) / cells
-    leave.wait()
 
     for phase in range(2):
         each_face(
@@ -270,16 +266,6 @@
         )
     for offset in range(1, group):
         heat_copy(offset).wait_send()
-
-
-def hand_on(block, result, done):
-    copies = [
-        pltpu.make_async_copy(block.at[x], result.at[x], done.at[x]) for x in range(block.shape[0])
-    ]
-    for copy in copies:
-        copy.start()
-    for copy in copies:
-        copy.wait()
 
 
 def local(
@@ -303,14 +289,14 @@
     hbm = pl.BlockSpec(memory_space=pl.ANY)
     single = jnp.float32
     flops = 4 * MAXSUB * cells * width * depth
-    advanced, worker_heat = pl.pallas_call(
+    return pl.pallas_call(
         kernel,
         out_shape=(
             jax.ShapeDtypeStruct(species.shape, single),
             jax.ShapeDtypeStruct((1, 1, 1), single),
         ),
         in_specs=[hbm] * 9,
-        out_specs=(hbm, vmem),
+        out_specs=(vmem, vmem),
         scratch_shapes=[
             pltpu.VMEM(species.shape, single),
             pltpu.VMEM((cy, cz, cx), counts.dtype),
@@ -330,43 +316,38 @@
             pltpu.VMEM(species.shape, single),
             pltpu.VMEM((cells, padded), single),
             pltpu.VMEM((cells, padded), single),
-            pltpu.VMEM(species.shape, single),
             pltpu.VMEM((cells, lanes), single),
             pltpu.VMEM((cells, lanes), single),
             pltpu.VMEM((1, lanes), single),
             pltpu.VMEM((group, 1, lanes), single),
-            pltpu.SemaphoreType.DMA((10,)),
+            pltpu.SemaphoreType.DMA((9,)),
             pltpu.SemaphoreType.DMA((2, 3, 2)),
             pltpu.SemaphoreType.DMA((2, 3, 2)),
             pltpu.SemaphoreType.DMA((group,)),
             pltpu.SemaphoreType.DMA((group,)),
         ],
         compiler_params=pltpu.CompilerParams(
-            collective_id=0, has_side_effects=True, vmem_limit_bytes=63 * 1024 * 1024
+            collective_id=0, has_side_effects=True, vmem_limit_bytes=48 * 1024 * 1024
         ),
         cost_estimate=pl.CostEstimate(
             flops=flops, bytes_accessed=5_000_000, transcendentals=2 * MAXSUB * cells * depth
         ),
     )(
-        species,
-        counts.transpose(1, 2, 0),
-        assignment.transpose(1, 2, 0),
-        cell_scale.transpose(1, 2, 0),
-        diffusivity,
-        order_weights,
-        stoichiometry.T,
-        rate_factor,
-        enthalpy,
-    )
-    result = pl.pallas_call(
-        hand_on,
-        out_shape=jax.ShapeDtypeStruct(species.shape, single),
-        in_specs=[hbm],
-        out_specs=hbm,
-        scratch_shapes=[pltpu.SemaphoreType.DMA((cx,))],
-        compiler_params=pltpu.CompilerParams(vmem_limit_bytes=63 * 1024 * 1024),
-    )(advanced)
-    return result, worker_heat
+        *(
+            pltpu.with_memory_space_constraint(operand, pltpu.HBM)
+            for operand in (
+                species,
+                counts.transpose(1, 2, 0),
+                assignment.transpose(1, 2, 0),
+                cell_scale.transpose(1, 2, 0),
+                diffusivity,
+                order_weights,
+                stoichiometry.T,
+                rate_factor,
+                enthalpy,
+            )
+        )
+    )
 
 
 def solution(mesh):

time: 41.4 us -> 29 us (0.70)
  Pallas kernels: 38.8 us -> 25.7 us
  local copies, waits for them, and re-layouts: 0 us -> 0.75 us
    pallas_call x1 -> x0, Pallas kernels: 13.1 us -> none  [local(): pl.pallas_call(hand_on, out_shape=jax.ShapeDtypeStruct(species.shape, sin...]
    unnamed x0 -> x1, local copies, waits for them, and re-layouts: none -> 0.75 us
where the time goes in v4:
time: 29 us; the launch traced here: 28.8 us
  Pallas kernels  25.7 us (89%)
  between operations  2.33 us (8%)
  local copies, waits for them, and re-layouts  0.75 us (3%)
    pallas_call x1, Pallas kernels, local(): pl.pallas_call(kernel, out_shape=(jax.ShapeDtypeStruct(species.shape, sin...  25.7 us
    unnamed x1, local copies, waits for them, and re-layouts  0.75 us

profile of v4, /device:TPU:0, one launch (start us, length us, event | category | flops | bytes accessed | tf_op | source)
XLA Modules:
  0.0 28.8 jit_solution(18388593983322989773)
XLA Ops:
  0.6 25.7 %shard_map.104 = (f32[8,4,4,654]{3,2,1,0:T(4,128)S(1)}, f32[1,1,1]{2,1,0:T(1,128)}) custom-call(f32[8,4,4,654]{3,2,1,0:T(4,128)} %refs_0_.1, s32[4,4,8]{2,1,0:T(4,128)} %bitcast.5, s32[4,4,8]{2,1,0:T(4,128)} %bitcast.6, f32[4,4,8]{2,1,0:T(4,128)} %bitcast.7, f32[654]{0:T(1024)} %refs_4_.1, bf16[654,1536]{1,0:T(8,128)(2,1)} %refs_5_.1, ...), custom_call_target="tpu_custom_call" | custom-call | flops 4114612224 | bytes 5000000 | tf_op jit(solution)/shard_map/pallas_call | solution.py:292
  26.4 0.7 %copy.13 = f32[8,4,4,654]{3,2,1,0:T(4,128)} copy(f32[8,4,4,654]{3,2,1,0:T(4,128)S(1)} %get-tuple-element.4) | data formatting | bytes 669696

commit v5 on v4

--- a/solution.py
+++ b/solution.py
@@ -203,18 +203,18 @@
                 preferred_element_type=jnp.float32,
             )
 
-        change = jnp.zeros((cells, padded), jnp.float32)
+        parts = []
         activity = activities(0)
         for first in range(0, depth, chunk):
             later = activities(first + chunk) if first + chunk < depth else None
             soft = jnp.maximum(activity, 0.0) + jnp.log(1.0 + jnp.exp(-jnp.abs(activity)))
-            rate_values = (factors[:, first : first + chunk] * soft).astype(jnp.bfloat16)
-            change = change + jnp.dot(
-                rate_values,
-                weights_turned[first : first + chunk, :],
-                preferred_element_type=jnp.float32,
-            )
+            parts.append((factors[:, first : first + chunk] * soft).astype(jnp.bfloat16))
             activity = later
+        change = jnp.dot(
+            jnp.concatenate(parts, axis=1),
+            weights_turned[...],
+            preferred_element_type=jnp.float32,
+        )
         now = rows[...]
         active = cell_counts[:, 0:1] > step.astype(jnp.float32)
         rows[...] = jnp.where(active, now + relax_rate * (change - now), now)

time: 29 us -> 27.7 us (0.955)
  Pallas kernels: 25.7 us -> 24.4 us
    pallas_call x1, Pallas kernels: 25.7 us -> 24.4 us  [local(): pl.pallas_call(kernel, out_shape=(jax.ShapeDtypeStruct(species.shape, sin...]
where the time goes in v5:
time: 27.7 us; the launch traced here: 27.5 us
  Pallas kernels  24.4 us (88%)
  between operations  2.33 us (8%)
  local copies, waits for them, and re-layouts  0.75 us (3%)
    pallas_call x1, Pallas kernels, local(): pl.pallas_call(kernel, out_shape=(jax.ShapeDtypeStruct(species.shape, sin...  24.4 us
    unnamed x1, local copies, waits for them, and re-layouts  0.75 us

profile of v5, /device:TPU:0, one launch (start us, length us, event | category | flops | bytes accessed | tf_op | source)
XLA Modules:
  0.0 27.5 jit_solution(13047764822797336995)
XLA Ops:
  0.6 24.4 %shard_map.104 = (f32[8,4,4,654]{3,2,1,0:T(4,128)S(1)}, f32[1,1,1]{2,1,0:T(1,128)}) custom-call(f32[8,4,4,654]{3,2,1,0:T(4,128)} %refs_0_.1, s32[4,4,8]{2,1,0:T(4,128)} %bitcast.5, s32[4,4,8]{2,1,0:T(4,128)} %bitcast.6, f32[4,4,8]{2,1,0:T(4,128)} %bitcast.7, f32[654]{0:T(1024)} %refs_4_.1, bf16[654,1536]{1,0:T(8,128)(2,1)} %refs_5_.1, ...), custom_call_target="tpu_custom_call" | custom-call | flops 4114612224 | bytes 5000000 | tf_op jit(solution)/shard_map/pallas_call | solution.py:292
  25.0 0.7 %copy.13 = f32[8,4,4,654]{3,2,1,0:T(4,128)} copy(f32[8,4,4,654]{3,2,1,0:T(4,128)S(1)} %get-tuple-element.4) | data formatting | bytes 669696
